TPU v7x, 512 devices: a whole 4x8x8 slice. The times are simulated.
512 devices in a mesh: feat: 16 (over x_hi, y), ex: 32 (over z, x_lo, core).
Axes of the slice: x: 4 (x_hi: 2, x_lo: 2; x = x_hi * 2 + x_lo), y: 8, z: 8, core: 2. Of those that a mesh axis runs over, the one named last changes fastest.
Arguments:
- train_grads: bfloat16 [4096, 262144], P('ex', 'feat')
- target_grads: bfloat16 [1024, 262144], P('ex', 'feat')
- signs: int32 [32, 8192], replicated, may hold values from -1 to 1, as said below
- block_order: int32 [32], replicated, may hold values from 0 to 31, each once
Outputs:
- train_features: bfloat16 [4096, 8192], P('ex', 'feat')
- cosines: float32 [4096, 32, 32], P('ex', None, 'feat')
Inputs may be any that keep to these rules, and one draw needn't show every extreme that they name: `signs`: every entry is +1 or -1.
All inputs are finite; a program needn't handle non-finite values.
Results may differ from a plain program's by a relative error of at most 0.013.
Values may be sent and summed in bfloat16 or wider, within the bound.
A program may use at most 64 MiB of HBM per device.

v0:
```python
import math

import jax
import jax.numpy as jnp
from jax import lax
from jax.sharding import PartitionSpec as P

HIN = 512


def sign_table(order_size):
    positions = jnp.arange(order_size, dtype=jnp.int32)
    parity = jnp.zeros((order_size, order_size), jnp.int32)
    for bit_place in range(order_size.bit_length() - 1):
        parity = parity + (positions[:, None] >> bit_place & 1) * (
            positions[None, :] >> bit_place & 1
        )
    return jnp.where(parity % 2 == 0, 1.0, -1.0).astype(jnp.float32)


def normalize(projected):
    widened = projected.astype(jnp.float32)
    row_scale = lax.rsqrt(jnp.mean(widened * widened, axis=-1, keepdims=True) + 1e-06)
    return (widened * row_scale).astype(jnp.bfloat16)


def local(train_grads, target_grads, signs, block_order):
    proj_width = signs.shape[1]
    block_total = signs.shape[0]
    blocks_here = train_grads.shape[1] // proj_width
    feat_count = lax.axis_size("feat")
    feat_index = lax.axis_index("feat")
    inner_size = HIN
    outer_size = proj_width // inner_size
    inner_table = sign_table(inner_size).astype(jnp.bfloat16)
    outer_table = sign_table(outer_size)
    positions_here = feat_index * blocks_here + jnp.arange(blocks_here, dtype=jnp.int32)
    selector = (block_order[None, :] == positions_here[:, None]).astype(jnp.float32)
    local_signs = jnp.dot(selector, signs.astype(jnp.float32)).astype(jnp.bfloat16)
    local_signs = local_signs.reshape(blocks_here, outer_size, inner_size)
    full_scale = 1.0 / math.sqrt(block_total * proj_width)

    def project_terms(gradients):
        row_count = gradients.shape[0]
        signed_blocks = (
            gradients.reshape(row_count, blocks_here, outer_size, inner_size) * local_signs[None]
        )
        inner_done = jnp.einsum(
            "rtoi,ij->roj", signed_blocks, inner_table, preferred_element_type=jnp.float32
        )
        outer_done = jnp.einsum(
            "roj,ok->rkj", inner_done, outer_table, precision=lax.Precision.HIGHEST
        )
        return outer_done.reshape(row_count, proj_width) * full_scale

    train_terms = project_terms(train_grads)
    target_terms = project_terms(target_grads)
    per_device = target_grads.shape[0] // feat_count
    dims_here = proj_width // feat_count
    group_count = lax.axis_size("ex")
    train_rows = train_grads.shape[0]
    train_sum, target_sum = lax.psum((train_terms, target_terms), "feat")
    train_full = train_sum.astype(jnp.bfloat16)
    target_full = target_sum.astype(jnp.bfloat16)
    target_mine = lax.dynamic_slice_in_dim(target_full, feat_index * per_device, per_device, 0)
    train_normed = normalize(train_full)
    train_features = lax.dynamic_slice_in_dim(train_normed, feat_index * dims_here, dims_here, 1)
    products = (
        jnp.einsum(
            "rp,kp->rk",
            train_normed,
            lax.all_gather(normalize(target_mine), "ex", axis=0, tiled=True),
            preferred_element_type=jnp.float32,
        )
        / proj_width
    )
    cosines = products.reshape(train_rows, group_count, per_device)
    return (train_features, cosines)


def solution(mesh):
    placed = (P("ex", "feat"), P("ex", "feat"), P(), P())
    return jax.shard_map(
        local,
        mesh=mesh,
        in_specs=placed,
        out_specs=(P("ex", "feat"), P("ex", None, "feat")),
        check_vma=False,
    )
```

profile of v0, /device:TPU:1, one launch (start us, length us, event | category | flops | bytes accessed | tf_op | source)
XLA Modules:
  0.0 235.6 jit_solution(5413964135909462783)
XLA Ops:
  7.2 0.0 all-gather.3.cloned.1.call-start
  7.3 1.5 convolution_convert_fusion
  8.8 1.6 copy.9
  10.4 0.3 convert_reduce_fusion.1
  10.6 1.5 fusion.6
  12.1 0.0 copy-start.1
  12.1 1.1 convolution_multiply_fusion.1
  13.2 0.6 copy.10
  13.8 0.5 copy-done.1
  14.3 1.7 copy.6
  16.0 1.4 convert_reduce_fusion
  17.4 1.9 fusion.8
  19.3 4.0 %convolution_multiply_fusion = f32[16,128,512]{2,0,1:T(8,128)S(1)} fusion(f32[128,16,512]{2,1,0:T(8,128)S(1)} %fusion.8, s32[16]{0:T(128)S(1)} %get-tuple-element.12, s32[16]{0:T(128)S(1)} %get-tuple-element.13, s32[16]{0:T(128)S(1)} %get-tuple-element.14, s32[16]{0:T(128)S(1)} %get-tuple-element.15), kind=kOutput, calls=%fused_computation.6 | convolution fusion | flops 202380288 | bytes 8388864 | tf_op jit(solution)/shard_map/roj,ok->rkj/dot_general | solution.py:51
  23.3 5.3 %copy.8 = f32[16,8,16,512]{3,1,2,0:T(8,128)} copy(f32[16,8,16,512]{3,2,1,0:T(8,128)S(1)} %bitcast.36) | data formatting | bytes 8388608
  28.7 121.5 %all-reduce.2 = (bf16[128,8192]{1,0:T(8,128)(2,1)S(1)}, bf16[32,8192]{1,0:T(8,128)(2,1)}) all-reduce(f32[128,8192]{1,0:T(8,128)} %bitcast.34, f32[32,8192]{1,0:T(8,128)S(1)} %bitcast.37), channel_id=1, replica_groups=mesh['feat'=16,'ex'=32] {'feat'}, use_global_device_ids=true, to_apply=%region_1.2 | all-reduce | flops 1310720 | bytes 7864320 | tf_op jit(solution)/shard_map/psum | solution.py:62
  150.2 0.0 copy-start
  150.2 1.3 fusion.10
  151.4 1.6 fusion.12
  153.1 0.0 all-gather.3.cloned.1.call-update
  153.1 0.5 fusion
  153.6 0.0 copy-done
  153.6 2.0 fusion.1
  155.6 0.7 constant_dynamic-slice_fusion
  156.3 69.5 %all-gather.3.cloned.1.call-done = bf16[32,2,8192]{2,1,0:T(2,128)(2,1)} async-done(((bf16[1,2,8192]{2,1,0:T(2,128)(2,1)}), bf16[32,2,8192]{2,1,0:T(2,128)(2,1)}) %all-gather.3.cloned.1.call-update) | async-done | bytes 1048592 | tf_op jit(solution)/shard_map/all_gather | solution.py:72
  225.8 1.5 reshape.227
  227.3 1.5 convolution_multiply_fusion.2
  (11 shorter events, 0.1 us)
Async XLA Ops:
  7.2 218.6 %all-gather.3.cloned.1.call-start = ((), (), s32[]{:S(2)}) async-start(), calls=%async_computation | async-start | bytes 1081344 | tf_op jit(solution)/shard_map/all_gather | solution.py:72
  12.1 2.2 copy-start.1
  150.2 3.4 %copy-start = (bf16[128,8192]{1,0:T(8,128)(2,1)}, bf16[128,8192]{1,0:T(8,128)(2,1)S(1)}, u32[]{:S(2)}) copy-start(bf16[128,8192]{1,0:T(8,128)(2,1)S(1)} %get-tuple-element.2) | copy-start | bytes 6291460
Sparse Core Ops, SparseCore 0:
  153.2 72.5 all-gather.2
where the time goes:
time: 236 us
  blocking collectives  122 us (52%)
  waiting for transfers between devices  69.5 us (29%)
  between operations  14.2 us (6%)
  local copies, waits for them, and re-layouts  11.9 us (5%)
  matrix products  11.3 us (5%)
  other arithmetic  7.08 us (3%)
    psum x1, blocking collectives, local(): train_sum, target_sum = lax.psum((train_terms, target_terms), 'feat')  122 us
    all_gather x1, waiting for transfers between devices, local(): lax.all_gather(normalize(target_mine), 'ex', axis=0, tiled=True)  69.5 us
    unnamed x10, local copies, waits for them, and re-layouts  11.2 us
    dot_general x2, matrix products, project_terms(): jnp.einsum('roj,ok->rkj', inner_done, outer_table, precision=lax.Precisio...  5.01 us
  transfers between devices with their start and end apart: 1, of which 1 were waited for; matrix products, arithmetic and copies ran while one was open for 1% of the time, Pallas kernels for 0%

commit v1 on v0

v1 whole, which is shorter than its diff:
```python
import functools

import jax
import jax.numpy as jnp
from jax import lax
from jax.experimental import pallas as pl
from jax.experimental.pallas import tpu as pltpu
from jax.sharding import PartitionSpec as P

MESH = pl.DeviceIdType.MESH
BF = jnp.bfloat16
F32 = jnp.float32

W = 512
PROJ = 8192
NF = 16
NY = 4
NX = 2
U = NY + NX
TRAIN = 16 * NY + 32 * NX
NT = (((1,), (1,)), ((), ()))
FAR_FIRST = (4, 3, 5, 2, 6, 1, 7)
PAIRS = ((0, 1), (7, 2), (6, 3), (5, 4))
ROUNDS = 2
PEERS = tuple((a, d) for d in (4, 3, 5, 2, 6, 1, 7, 0) for a in (1, 0) if (a, d) != (0, 0))


def butterfly(values):
    span = 1
    while span < len(values):
        out = list(values)
        for i in range(len(values)):
            if not i & span:
                out[i] = values[i] + values[i + span]
                out[i + span] = values[i] - values[i + span]
        values = out
        span *= 2
    return values


def kernel(
    train_hbm, target_hbm, signs_hbm, order_ref,
    feat_out, cos_out,
    tr_v, tg_v, sg_v, lsig, had, perm,
    mt, rxt, rcvt, my, mx, rxx, rcv, zs, rzs, tall, proj, stat, rstat, part, rpart,
    ld, tx_s, tx_r, xx_s, xx_r, ty_s, ty_r, it_s, it_r, yx_s, yx_r, xl_s, xl_r, zz_s, zz_r, cc_s, cc_r, st_s, st_r, co_s, co_r,
):
    f = lax.axis_index("feat")
    e = lax.axis_index("ex")
    h, y = f // 8, f % 8
    z, xl, c = e // 4, (e // 2) % 2, e % 2
    oh = 1 - h

    def on_feat(a, d):
        return (((h + a) % 2) * 8 + (y + d) % 8, e)

    def on_z(d):
        return (f, ((z + d) % 8) * 4 + xl * 2 + c)

    xl_dev = (f, z * 4 + (1 - xl) * 2 + c)
    core_dev = (f, z * 4 + xl * 2 + (1 - c))

    def remote(src, dst, s, r, dev):
        return pltpu.make_async_remote_copy(
            src_ref=src, dst_ref=dst, send_sem=s, recv_sem=r, device_id=dev, device_id_type=MESH
        )

    barrier = pltpu.get_barrier_semaphore()
    partners = [on_feat(a, d) for a, d in PEERS] + [on_z(d) for d in range(1, 8)] + [xl_dev, core_dev]
    for dev in partners:
        pl.semaphore_signal(barrier, inc=1, device_id=dev, device_id_type=MESH)

    loads = [
        pltpu.make_async_copy(signs_hbm, sg_v, ld.at[0]),
        pltpu.make_async_copy(target_hbm, tg_v, ld.at[1]),
    ]
    for u in range(U):
        lo, n = (16 * u, 16) if u < NY else (16 * NY + 32 * (u - NY), 32)
        loads.append(
            pltpu.make_async_copy(train_hbm.at[pl.ds(lo, n)], tr_v.at[pl.ds(lo, n)], ld.at[2 + u])
        )
    for load in loads:
        load.start()

    parity = lax.broadcasted_iota(jnp.int32, (W, W), 0) & lax.broadcasted_iota(jnp.int32, (W, W), 1)
    for shift in (8, 4, 2, 1):
        parity = parity ^ (parity >> shift)
    had[...] = (1 - 2 * (parity & 1)).astype(F32).astype(BF)
    n_out = lax.broadcasted_iota(jnp.int32, (256, 256), 0)
    n_in = lax.broadcasted_iota(jnp.int32, (256, 256), 1)
    wanted = (
        ((n_out >> 3) & 1) * 128 + ((n_out >> 1) & 1) * 64 + ((n_out >> 2) & 1) * 32 + (n_out >> 4) * 2 + (n_out & 1)
    )
    perm[...] = jnp.where(wanted == n_in, 1.0, 0.0).astype(BF)

    loads[0].wait()
    slot = lax.broadcasted_iota(jnp.int32, (8, 32), 0)
    chosen = (order_ref[...] == f * 2 + slot) & (slot < 2)
    lsig[...] = jnp.dot(
        jnp.where(chosen, 1.0, 0.0).astype(BF),
        sg_v[...].astype(F32).astype(BF),
        preferred_element_type=F32,
    )

    def premix(grads, row, store):
        def tile(t, carry):
            values = []
            for b in range(NF):
                at0 = pl.ds(pl.multiple_of(b * W + t * 128, 128), 128)
                at1 = pl.ds(pl.multiple_of(PROJ + b * W + t * 128, 128), 128)
                g0 = grads[pl.ds(row, 16), at0].astype(F32)
                g1 = grads[pl.ds(row, 16), at1].astype(F32)
                values.append(g0 * lsig[pl.ds(0, 1), at0] + g1 * lsig[pl.ds(1, 1), at0])
            lanes = pl.ds(pl.multiple_of(t * 128, 128), 128)
            for dest, value in enumerate(butterfly(values)):
                store(dest, lanes, value.astype(BF))
            return carry

        lax.fori_loop(0, W // 128, tile, 0)

    def store_split(buf, k):
        def store(dest, lanes, value):
            buf[dest // 8, dest % 8, pl.ds(16 * k, 16), lanes] = value

        return store

    def store_y(u):
        def store(dest, lanes, value):
            my[u, dest % 8, pl.ds(16 * (dest // 8), 16), lanes] = value

        return store

    def yy(d):
        return (y + d) % 8

    tx = {d: remote(mt.at[oh, yy(d)], rxt.at[yy(d)], tx_s.at[d], tx_r.at[d], on_feat(1, 0)) for d in range(8)}
    xx = {
        (u, d): remote(mx.at[u, oh, yy(d)], rxx.at[u, yy(d)], xx_s.at[u, d], xx_r.at[u, d], on_feat(1, 0))
        for u in range(NX)
        for d in range(8)
    }
    ty = {d: remote(mt.at[h, yy(d)], rcvt.at[d - 1], ty_s.at[d - 1], ty_r.at[d - 1], on_feat(0, d)) for d in range(1, 8)}

    def own(u, d):
        return my.at[u, yy(d)] if u < NY else mx.at[u - NY, h, yy(d)]

    it = {}
    for u in range(U):
        for way, sign in ((0, 1), (1, -1)):
            for s in range(4):
                rows = pl.ds(16 * way, 16) if s == 0 else pl.ds(0, 32)
                it[u, way, s] = remote(
                    own(u, sign * (4 - s) + 8).at[rows],
                    rcv.at[u, way, s, rows],
                    it_s.at[u, way, s],
                    it_r.at[u, way, s],
                    on_feat(0, sign + 8),
                )
    yx = {u: remote(zs.at[u, oh], rzs.at[u], yx_s.at[u], yx_r.at[u], on_feat(1, 0)) for u in range(NY)}
    own_t = tall.at[0, c, xl]
    other_t = tall.at[0, c, 1 - xl]
    xlc = remote(own_t, own_t, xl_s, xl_r, xl_dev)
    zz = {}
    for d in range(1, 8):
        zz[0, d] = remote(own_t, tall.at[8 - d, c, xl], zz_s.at[0, 8 - d], zz_r.at[0, 8 - d], on_z(d))
        zz[1, d] = remote(other_t, tall.at[8 - d, c, 1 - xl], zz_s.at[1, 8 - d], zz_r.at[1, 8 - d], on_z(d))
    cc = {d: remote(tall.at[d, c], tall.at[d, c], cc_s.at[d], cc_r.at[d], core_dev) for d in range(8)}
    st = {
        j: remote(stat, rstat.at[j], st_s.at[j], st_r.at[j], on_feat(a, d)) for j, (a, d) in enumerate(PEERS)
    }
    co = {}
    for r in range(ROUNDS):
        rows = pl.ds(32 * r, 32 if r + 1 < ROUNDS else 48)
        for j, (a, d) in enumerate(PEERS):
            dev = on_feat(a, d)
            co[r, j] = remote(part.at[dev[0], rows], rpart.at[j, rows], co_s.at[r, j], co_r.at[r, j], dev)

    sent = []

    def start(copy):
        copy.start()
        sent.append(copy)

    def add(to, rows, arrived):
        to[rows] = (to[rows].astype(F32) + arrived.astype(F32)).astype(BF)

    every = pl.ds(0, 32)

    def step(u, s):
        for way, sign in ((0, 1), (1, -1)):
            to = own(u, sign * (4 - s) + 8)
            if u >= NY:
                xu = u - NY
                d = (sign * (4 - s) + 8) % 8
                if s > 0 or way == 0:
                    xx[xu, d].wait_recv()
                    add(to, every, rxx[xu, yy(d)])
            if s > 0:
                it[u, way, s - 1].wait_recv()
                rows = pl.ds(16 * way, 16) if s == 1 else every
                add(to, rows, rcv[u, way, s - 1, rows])
            start(it[u, way, s])

    def transform(rows_sum, row, n):
        high = rows_sum.astype(BF)
        low = (rows_sum - high.astype(F32)).astype(BF)
        table = had[...]
        done = jnp.dot(high, table, preferred_element_type=F32) + jnp.dot(low, table, preferred_element_type=F32)
        return (done * (2.0**-9)).astype(BF)

    def gather_step(u):
        if u >= NY:
            xx[u - NY, 0].wait_recv()
        it[u, 0, 3].wait_recv()
        it[u, 1, 3].wait_recv()
        total = own(u, 0)[...].astype(F32) + rcv[u, 0, 3].astype(F32) + rcv[u, 1, 3].astype(F32)
        if u >= NY:
            return total + rxx[u - NY, yy(0)].astype(F32)
        return total

    def finish_y_send(u):
        total = gather_step(u)
        zs[u] = total.reshape(2, 16, W).astype(BF)
        start(yx[u])

    def finish_y(u):
        yx[u].wait_recv()
        total = zs[u, h].astype(F32) + rzs[u].astype(F32)
        proj[pl.ds(16 * u, 16)] = transform(total, 16 * u, 16)

    def finish_x(u):
        row = 16 * NY + 32 * (u - NY)
        proj[pl.ds(row, 32)] = transform(gather_step(u), row, 32)

    def target_step(d):
        tx[d].wait_recv()
        add(mt.at[h, yy(d)], every, rxt[yy(d)])
        start(ty[d])

    def target_finish():
        tx[0].wait_recv()
        total = mt[h, y].astype(F32) + rxt[yy(0)].astype(F32)
        for d in FAR_FIRST:
            ty[d].wait_recv()
            total = total + rcvt[d - 1].astype(F32)
        tall[0, c, xl] = transform(total, 0, 32)
        start(xlc)
        for d in FAR_FIRST:
            start(zz[0, d])

    def target_second():
        xlc.wait_recv()
        for d in FAR_FIRST:
            start(zz[1, d])
        start(cc[0])

    def forward(d):
        zz[0, 8 - d].wait_recv()
        zz[1, 8 - d].wait_recv()
        start(cc[d])

    loads[1].wait()
    for k in range(2):
        premix(tg_v, 16 * k, store_split(mt, k))
    pl.semaphore_wait(barrier, len(partners))
    for d in FAR_FIRST + (0,):
        start(tx[d])
    for u in range(NY):
        loads[2 + u].wait()
        premix(tr_v, 16 * u, store_y(u))
        step(u, 0)
    for u in range(NX):
        loads[2 + NY + u].wait()
        for k in range(2):
            premix(tr_v, 16 * NY + 32 * u + 16 * k, store_split(mx.at[u], k))
    for d in FAR_FIRST + (0,):
        for u in range(NX):
            start(xx[u, d])

    queue = list(FAR_FIRST)
    for u in range(NY):
        target_step(queue.pop(0))
        step(u, 1)
    for d in queue:
        target_step(d)
    for u in range(NY):
        step(u, 2)
    for u in range(NX):
        step(NY + u, 0)
    target_finish()
    for u in range(NY):
        step(u, 3)
    for u in range(NX):
        step(NY + u, 1)
    target_second()
    for u in range(NX):
        step(NY + u, 2)
    for u in range(NY):
        finish_y_send(u)
    for u in range(NX):
        step(NY + u, 3)
    for u in range(NY):
        finish_y(u)
    for u in range(NX):
        finish_x(NY + u)

    wide = proj[...].astype(F32)
    square = wide * wide
    high = square.astype(BF)
    low = (square - high.astype(F32)).astype(BF)
    ones = jnp.ones((8, W), BF)
    stat[...] = lax.dot_general(ones, high, NT, preferred_element_type=F32) + lax.dot_general(
        ones, low, NT, preferred_element_type=F32
    )
    for j in range(len(PEERS)):
        start(st[j])
    for pair in PAIRS[:2]:
        for d in pair:
            if d:
                forward(d)
    total = stat[...]
    for j in range(len(PEERS)):
        st[j].wait_recv()
        total = total + rstat[j]
    scale = lax.rsqrt(total[0:1] * (1.0 / PROJ) + 1e-06)
    eye = lax.broadcasted_iota(jnp.int32, (TRAIN, TRAIN), 0) == lax.broadcasted_iota(jnp.int32, (TRAIN, TRAIN), 1)
    column = jnp.sum(jnp.where(eye, scale, 0.0), axis=1, keepdims=True)
    proj[...] = (proj[...].astype(F32) * column).astype(BF)
    feat_out[...] = proj[...]

    lane = lax.broadcasted_iota(jnp.int32, (256, 128), 1)
    squares = jnp.zeros((256, 128), F32)
    for k, pair in enumerate(PAIRS):
        if k >= 2:
            for d in pair:
                forward(d)
        for d in pair:
            cc[d].wait_recv()
        rows = jnp.concatenate([tall[d].reshape(128, W) for d in pair], axis=0)
        products = lax.dot_general(rows, proj[...], NT, preferred_element_type=F32).astype(BF)
        ordered = jnp.dot(perm[...], products, preferred_element_type=F32).astype(BF)
        part[:, pl.ds(16 * k, 16), :] = ordered.reshape(NF, 16, TRAIN)
        wide = rows.astype(F32)
        norm = jnp.sum(wide * wide, axis=1, keepdims=True)
        norm_high = norm.astype(BF).astype(F32)
        squares = squares + jnp.where(lane == 2 * k, norm_high, 0.0) + jnp.where(lane == 2 * k + 1, norm - norm_high, 0.0)
        if k == len(PAIRS) - 1:
            moved = jnp.dot(perm[...], squares.astype(BF), preferred_element_type=F32).astype(BF)
            part[:, pl.ds(64, 16), :] = moved.reshape(NF, 16, 128)
        if k % 2 == 1:
            for j in range(len(PEERS)):
                start(co[k // 2, j])

    total = part[f].astype(F32)
    for j in range(len(PEERS)):
        for r in range(ROUNDS):
            co[r, j].wait_recv()
        total = total + rpart[j].astype(F32)
    lane16 = lax.broadcasted_iota(jnp.int32, (16, 128), 1)
    for k, pair in enumerate(PAIRS):
        norm = jnp.sum(jnp.where(lane16 // 2 == k, total[64:80], 0.0), axis=1, keepdims=True)
        factor = lax.rsqrt(norm * (1.0 / PROJ) + 1e-06) * (1.0 / PROJ)
        block = total[16 * k : 16 * k + 16] * factor
        for i, d in enumerate(pair):
            cos_out[pl.ds(pl.multiple_of(((z + d) % 8) * 8, 8), 8), :] = block[8 * i : 8 * i + 8]

    for copy in sent:
        copy.wait_send()


def solution(mesh):
    vm = pltpu.VMEM
    dma = pltpu.SemaphoreType.DMA
    n_peers = len(PEERS)
    scratch = [
        vm((TRAIN, 2 * PROJ), BF), vm((32, 2 * PROJ), BF), vm((32, PROJ), jnp.int32), vm((8, PROJ), F32),
        vm((W, W), BF), vm((256, 256), BF),
        vm((2, 8, 32, W), BF), vm((8, 32, W), BF), vm((7, 32, W), BF),
        vm((NY, 8, 32, W), BF), vm((NX, 2, 8, 32, W), BF), vm((NX, 8, 32, W), BF), vm((U, 2, 4, 32, W), BF),
        vm((NY, 2, 16, W), BF), vm((NY, 16, W), BF),
        vm((8, 2, 2, 32, W), BF), vm((TRAIN, W), BF),
        vm((8, 128), F32), vm((n_peers, 8, 128), F32),
        vm((NF, 80, 128), BF), vm((n_peers, 80, 128), BF),
        dma((2 + U,)), dma((8,)), dma((8,)), dma((NX, 8)), dma((NX, 8)), dma((7,)), dma((7,)),
        dma((U, 2, 4)), dma((U, 2, 4)), dma((NY,)), dma((NY,)), dma, dma, dma((2, 8)), dma((2, 8)),
        dma((8,)), dma((8,)), dma((n_peers,)), dma((n_peers,)), dma((ROUNDS, n_peers)), dma((ROUNDS, n_peers)),
    ]
    hbm = pl.BlockSpec(memory_space=pl.ANY)
    whole = pl.BlockSpec(memory_space=pltpu.VMEM)

    def local(train_grads, target_grads, signs, block_order):
        features, cosines = pl.pallas_call(
            kernel,
            out_shape=(
                jax.ShapeDtypeStruct((TRAIN, W), BF),
                jax.ShapeDtypeStruct((64, 128), F32),
            ),
            in_specs=[hbm, hbm, hbm, whole],
            out_specs=(whole, whole),
            scratch_shapes=scratch,
            compiler_params=pltpu.CompilerParams(
                collective_id=0, has_side_effects=True, vmem_limit_bytes=48 * 2**20
            ),
        )(train_grads, target_grads, signs, block_order.reshape(1, 32))
        return features, cosines.reshape(32, 2, TRAIN).transpose(2, 0, 1)

    placed = (P("ex", "feat"), P("ex", "feat"), P(), P())
    return jax.shard_map(
        local,
        mesh=mesh,
        in_specs=placed,
        out_specs=(P("ex", "feat"), P("ex", None, "feat")),
        check_vma=False,
    )
```

time: 236 us -> 68.9 us (0.29)
  blocking collectives: 122 us -> 0 us
  waiting for transfers between devices: 69.5 us -> 0 us
  Pallas kernels: 0 us -> 63.7 us
  between operations: 14.2 us -> 0.65 us
  matrix products: 11.3 us -> 0 us
  local copies, waits for them, and re-layouts: 11.9 us -> 4.37 us
  other arithmetic: 7.08 us -> 0 us
    psum x1 -> x0, blocking collectives: 122 us -> none  [local(): train_sum, target_sum = lax.psum((train_terms, target_terms), 'feat')]
    all_gather x1 -> x0, waiting for transfers between devices: 69.5 us -> none  [local(): lax.all_gather(normalize(target_mine), 'ex', axis=0, tiled=True)]
    pallas_call x0 -> x1, Pallas kernels: none -> 63.7 us  [local(): pl.pallas_call(kernel, out_shape=(jax.ShapeDtypeStruct((TRAIN, W), BF), j...]
    dot_general x6 -> x0, matrix products: 11.3 us -> none  [the longest x2 5.01 us: project_terms(): jnp.einsum('roj,ok->rkj', inner_done, outer_table, precision=lax.Precisio...]
    unnamed x10 -> x8, local copies, waits for them, and re-layouts: 11.2 us -> 4.37 us
    reduce_sum x4 -> x0, other arithmetic: 3.38 us -> none  [the longest x2 1.75 us: normalize(): jnp.mean(widened * widened, axis=-1, keepdims=True) + 1e-06]
  transfers between devices with their start and end apart: 1 -> 0, of which waited for: 1 -> 0; matrix products, arithmetic and copies ran while one was open for 1% -> 0% of each run, Pallas kernels for 0% -> 0%
where the time goes in v1:
time: 68.9 us; the launch traced here: 68.7 us
  Pallas kernels  63.7 us (92%)
  local copies, waits for them, and re-layouts  4.37 us (6%)
    pallas_call x1, Pallas kernels, local(): pl.pallas_call(kernel, out_shape=(jax.ShapeDtypeStruct((TRAIN, W), BF), j...  63.7 us
    unnamed x8, local copies, waits for them, and re-layouts  4.37 us

profile of v1, /device:TPU:1, one launch (start us, length us, event | category | flops | bytes accessed | tf_op | source)
XLA Modules:
  0.0 68.7 jit_solution(11516891806414937246)
XLA Ops:
  0.6 0.0 copy-start
  0.6 1.2 %copy-done = bf16[32,16384]{1,0:T(8,128)(2,1)S(1)} copy-done((bf16[32,16384]{1,0:T(8,128)(2,1)S(1)}, bf16[32,16384]{1,0:T(8,128)(2,1)}, u32[]{:S(2)}) %copy-start) | copy-done | bytes 1048600
  1.9 0.0 copy-start.1
  1.9 1.2 %copy-done.1 = s32[32,8192]{1,0:T(8,128)S(1)} copy-done((s32[32,8192]{1,0:T(8,128)S(1)}, s32[32,8192]{1,0:T(8,128)}, u32[]{:S(2)}) %copy-start.1) | copy-done | bytes 1048600
  3.1 0.0 copy-start.2
  3.1 0.7 copy-done.2
  3.7 63.7 %shard_map.59 = (bf16[128,512]{1,0:T(8,128)(2,1)S(1)}, f32[64,128]{1,0:T(8,128)S(1)}) custom-call(bf16[128,16384]{1,0:T(8,128)(2,1)} %train_hbm.1, bf16[32,16384]{1,0:T(8,128)(2,1)S(1)} %copy-done, s32[32,8192]{1,0:T(8,128)S(1)} %copy-done.1, s32[1,32]{1,0:T(1,128)S(1)} %bitcast.5), custom_call_target="tpu_custom_call" | custom-call | tf_op jit(solution)/shard_map/pallas_call | solution.py:392
  67.5 0.7 copy.8
  68.1 0.6 copy.9
Async XLA Ops:
  0.6 1.2 %copy-start = (bf16[32,16384]{1,0:T(8,128)(2,1)S(1)}, bf16[32,16384]{1,0:T(8,128)(2,1)}, u32[]{:S(2)}) copy-start(bf16[32,16384]{1,0:T(8,128)(2,1)} %target_hbm.1) | copy-start | bytes 3145732
  1.9 1.2 %copy-start.1 = (s32[32,8192]{1,0:T(8,128)S(1)}, s32[32,8192]{1,0:T(8,128)}, u32[]{:S(2)}) copy-start(s32[32,8192]{1,0:T(8,128)} %signs_hbm.1) | copy-start | bytes 3145732
  3.1 0.7 copy-start.2

commit v2 on v1

v2 whole, which is shorter than its diff:
```python
import functools

import jax
import jax.numpy as jnp
from jax import lax
from jax.experimental import pallas as pl
from jax.experimental.pallas import tpu as pltpu
from jax.sharding import PartitionSpec as P

MESH = pl.DeviceIdType.MESH
BF = jnp.bfloat16
F32 = jnp.float32

W = 512
PROJ = 8192
VML = 53.4
NF = 16
NY = 4
NX = 2
U = NY + NX
TRAIN = 16 * NY + 32 * NX
NT = (((1,), (1,)), ((), ()))
FAR_FIRST = (4, 3, 5, 2, 6, 1, 7)
PAIRS = ((0, 4), (3, 5), (2, 6), (1, 7))
GROUPS = ((0, 1, 2), (3,))
ROUNDS = len(GROUPS)
PEERS = tuple((a, d) for d in (4, 3, 5, 2, 6, 1, 7, 0) for a in (1, 0) if (a, d) != (0, 0))


def butterfly(values):
    span = 1
    while span < len(values):
        out = list(values)
        for i in range(len(values)):
            if not i & span:
                out[i] = values[i] + values[i + span]
                out[i + span] = values[i] - values[i + span]
        values = out
        span *= 2
    return values


def kernel(
    train_hbm, target_hbm, signs_hbm, order_ref,
    feat_out, cos_out,
    tr_v, tg_v, sg_v, lsig, had, perm,
    mt, rt4, rt, zt, rzt, my, mx, rxx, rcv, zs, rzs, tall, proj, stat, rstat, part, rpart,
    ld, xx_s, xx_r, ty_s, ty_r, it_s, it_r, yx_s, yx_r, tq_s, tq_r, zz_s, zz_r, cc_s, cc_r, st_s, st_r, co_s, co_r, far_z,
):
    f = lax.axis_index("feat")
    e = lax.axis_index("ex")
    h, y = f // 8, f % 8
    z, xl, c = e // 4, (e // 2) % 2, e % 2
    oh = 1 - h

    def on_feat(a, d):
        return (((h + a) % 2) * 8 + (y + d) % 8, e)

    def on_z(d):
        return (f, ((z + d) % 8) * 4 + xl * 2 + c)

    across = [(f, z * 4 + (1 - xl) * 2 + c), on_feat(1, 0), (oh * 8 + y, z * 4 + (1 - xl) * 2 + c)]
    core_dev = (f, z * 4 + xl * 2 + (1 - c))

    def remote(src, dst, s, r, dev):
        return pltpu.make_async_remote_copy(
            src_ref=src, dst_ref=dst, send_sem=s, recv_sem=r, device_id=dev, device_id_type=MESH
        )

    loads = [
        pltpu.make_async_copy(signs_hbm, sg_v, ld.at[0]),
        pltpu.make_async_copy(target_hbm.at[pl.ds(0, 16)], tg_v.at[pl.ds(0, 16)], ld.at[1]),
        pltpu.make_async_copy(target_hbm.at[pl.ds(16, 16)], tg_v.at[pl.ds(16, 16)], ld.at[2]),
    ]
    for u in range(U):
        lo, n = (16 * u, 16) if u < NY else (16 * NY + 32 * (u - NY), 32)
        loads.append(
            pltpu.make_async_copy(train_hbm.at[pl.ds(lo, n)], tr_v.at[pl.ds(lo, n)], ld.at[3 + u])
        )
    for load in loads[:3]:
        load.start()

    barrier = pltpu.get_barrier_semaphore()
    partners = [on_feat(0, d) for d in (2, 6, 1, 7)] + across + [on_z(d) for d in (2, 6, 1, 7)] + [core_dev]
    for dev in partners:
        pl.semaphore_signal(barrier, inc=1, device_id=dev, device_id_type=MESH)

    loads[0].wait()
    slot = lax.broadcasted_iota(jnp.int32, (8, 32), 0)
    chosen = (order_ref[...] == f * 2 + slot) & (slot < 2)
    lsig[...] = jnp.dot(
        jnp.where(chosen, 1.0, 0.0).astype(BF),
        sg_v[...].astype(F32).astype(BF),
        preferred_element_type=F32,
    )

    def tables():
        parity = lax.broadcasted_iota(jnp.int32, (W, W), 0) & lax.broadcasted_iota(jnp.int32, (W, W), 1)
        for shift in (8, 4, 2, 1):
            parity = parity ^ (parity >> shift)
        had[...] = (1 - 2 * (parity & 1)).astype(F32).astype(BF)
        n_out = lax.broadcasted_iota(jnp.int32, (256, 256), 0)
        n_in = lax.broadcasted_iota(jnp.int32, (256, 256), 1)
        wanted = (
            ((n_out >> 3) & 1) * 128
            + ((n_out >> 1) & 1) * 64
            + (n_out >> 7) * 32
            + ((n_out >> 2) & 1) * 16
            + ((n_out >> 4) & 7) * 2
            + (n_out & 1)
        )
        perm[...] = jnp.where(wanted == n_in, 1.0, 0.0).astype(BF)

    def premix(grads, row, store):
        def tile(t, carry):
            values = []
            for b in range(NF):
                at0 = pl.ds(pl.multiple_of(b * W + t * 128, 128), 128)
                at1 = pl.ds(pl.multiple_of(PROJ + b * W + t * 128, 128), 128)
                g0 = grads[pl.ds(row, 16), at0].astype(F32)
                g1 = grads[pl.ds(row, 16), at1].astype(F32)
                values.append(g0 * lsig[pl.ds(0, 1), at0] + g1 * lsig[pl.ds(1, 1), at0])
            lanes = pl.ds(pl.multiple_of(t * 128, 128), 128)
            for dest, value in enumerate(butterfly(values)):
                store(dest, lanes, value.astype(BF))
            return carry

        lax.fori_loop(0, W // 128, tile, 0)

    def store_split(buf, k):
        def store(dest, lanes, value):
            buf[dest // 8, dest % 8, pl.ds(16 * k, 16), lanes] = value

        return store

    def store_y(buf):
        def store(dest, lanes, value):
            buf[dest % 8, pl.ds(16 * (dest // 8), 16), lanes] = value

        return store

    def yy(d):
        return (y + d) % 8

    xx = {
        (u, d): remote(mx.at[u, oh, yy(d)], rxx.at[u, yy(d)], xx_s.at[u, d], xx_r.at[u, d], on_feat(1, 0))
        for u in range(NX)
        for d in range(8)
    }
    ty = {}
    for k in range(2):
        for way, sign in ((0, 1), (1, -1)):
            rows = pl.ds(16 * way, 16)
            for name, apart, hops in ((3, 3, 1), (1, 1, 1), (2, 2, 2)):
                ty[k, way, name] = remote(
                    mt.at[k, yy(8 + sign * apart)], rt.at[k, way, name - 1],
                    ty_s.at[k, way, name - 1], ty_r.at[k, way, name - 1], on_feat(0, 8 + sign * hops),
                )
            ty[k, way, 4] = remote(
                mt.at[k, yy(4), rows], rt4.at[k, way], ty_s.at[k, way, 3], ty_r.at[k, way, 3], on_feat(0, 8 + 2 * sign)
            )
    tq = {
        (k, i): remote(zt.at[k, h if i == 0 else oh], rzt.at[k, i], tq_s.at[k, i], tq_r.at[k, i], across[i])
        for k in range(2)
        for i in range(3)
    }

    def own(u, d):
        return my.at[u, yy(d)] if u < NY else mx.at[u - NY, h, yy(d)]

    it = {}
    for u in range(U):
        for way, sign in ((0, 1), (1, -1)):
            for s in range(4):
                rows = pl.ds(16 * way, 16) if s == 0 else pl.ds(0, 32)
                it[u, way, s] = remote(
                    own(u, sign * (4 - s) + 8).at[rows],
                    rcv.at[u, way, s, rows],
                    it_s.at[u, way, s],
                    it_r.at[u, way, s],
                    on_feat(0, sign + 8),
                )
    yx = {u: remote(zs.at[u, oh], rzs.at[u], yx_s.at[u], yx_r.at[u], on_feat(1, 0)) for u in range(NY)}
    zz = {
        (k, d): remote(
            tall.at[0, c, k], tall.at[8 - d, c, k], zz_s.at[k, 8 - d], zz_r.at[k, 8 - d], on_z(d)
        )
        for k in range(2)
        for d in range(1, 8)
    }
    cc = {d: remote(tall.at[d, c], tall.at[d, c], cc_s.at[d], cc_r.at[d], core_dev) for d in range(8)}
    st = {
        j: remote(stat, rstat.at[j], st_s.at[j], st_r.at[j], on_feat(a, d)) for j, (a, d) in enumerate(PEERS)
    }
    co = {}
    for r in range(ROUNDS):
        rows = pl.ds(16 * GROUPS[r][0], 16 * len(GROUPS[r]) + (0 if r + 1 < ROUNDS else 16))
        for j, (a, d) in enumerate(PEERS):
            dev = on_feat(a, d)
            co[r, j] = remote(part.at[dev[0], rows], rpart.at[j, rows], co_s.at[r, j], co_r.at[r, j], dev)

    sent = []

    def start(copy):
        copy.start()
        sent.append(copy)

    def add(to, rows, arrived):
        to[rows] = (to[rows].astype(F32) + arrived.astype(F32)).astype(BF)

    every = pl.ds(0, 32)

    def step(u, s):
        for way, sign in ((0, 1), (1, -1)):
            to = own(u, sign * (4 - s) + 8)
            if u >= NY:
                xu = u - NY
                d = (sign * (4 - s) + 8) % 8
                if s > 0 or way == 0:
                    xx[xu, d].wait_recv()
                    add(to, every, rxx[xu, yy(d)])
            if s > 0:
                it[u, way, s - 1].wait_recv()
                rows = pl.ds(16 * way, 16) if s == 1 else every
                add(to, rows, rcv[u, way, s - 1, rows])
            start(it[u, way, s])

    def transform(rows_sum):
        high = rows_sum.astype(BF)
        low = (rows_sum - high.astype(F32)).astype(BF)
        table = had[...]
        done = jnp.dot(high, table, preferred_element_type=F32) + jnp.dot(low, table, preferred_element_type=F32)
        return (done * (2.0**-9)).astype(BF)

    def gather_step(u):
        if u >= NY:
            xx[u - NY, 0].wait_recv()
        it[u, 0, 3].wait_recv()
        it[u, 1, 3].wait_recv()
        total = own(u, 0)[...].astype(F32) + rcv[u, 0, 3].astype(F32) + rcv[u, 1, 3].astype(F32)
        if u >= NY:
            return total + rxx[u - NY, yy(0)].astype(F32)
        return total

    def finish_y_send(u):
        total = gather_step(u)
        zs[u] = total.reshape(2, 16, W).astype(BF)
        start(yx[u])

    def finish_y(u):
        yx[u].wait_recv()
        total = zs[u, h].astype(F32) + rzs[u].astype(F32)
        proj[pl.ds(16 * u, 16)] = transform(total)

    def finish_x(u):
        row = 16 * NY + 32 * (u - NY)
        proj[pl.ds(row, 32)] = transform(gather_step(u))

    def target_one(k):
        for name in (4, 3, 1):
            for way in range(2):
                start(ty[k, way, name])

    def target_two(k):
        for way, sign in ((0, 1), (1, -1)):
            to = mt.at[k, yy(8 + 2 * sign)]
            ty[k, way, 3].wait_recv()
            ty[k, way, 4].wait_recv()
            add(to, every, rt[k, way, 2])
            add(to, pl.ds(16 * way, 16), rt4[k, way])
            start(ty[k, way, 2])

    def target_across(k):
        total = mt[k, y].astype(F32)
        for name in (1, 2):
            for way in range(2):
                ty[k, way, name].wait_recv()
                total = total + rt[k, way, name - 1].astype(F32)
        zt[k] = total.reshape(2, 16, W).astype(BF)
        for i in (1, 2, 0):
            start(tq[k, i])

    def target_finish(k):
        for i in range(3):
            tq[k, i].wait_recv()
        mine = zt[k, h].astype(F32) + rzt[k, 1].astype(F32)
        other = rzt[k, 0].astype(F32) + rzt[k, 2].astype(F32)
        done = transform(jnp.concatenate([mine, other], axis=0))
        tall[0, c, k, xl] = done[0:16]
        tall[0, c, k, 1 - xl] = done[16:32]
        for d in FAR_FIRST:
            start(zz[k, d])

    def send_x(u, distances):
        for d in distances:
            start(xx[u, d])

    def forward(d):
        zz[0, 8 - d].wait_recv()
        zz[1, 8 - d].wait_recv()
        start(cc[d])

    loads[1].wait()
    for load in loads[3:]:
        load.start()
    premix(tg_v, 0, store_y(mt.at[0]))
    pl.semaphore_wait(barrier, len(partners))
    target_one(0)
    for d in (2, 6):
        pl.semaphore_signal(far_z, inc=1, device_id=on_z(d), device_id_type=MESH)
    loads[2].wait()
    premix(tg_v, 16, store_y(mt.at[1]))
    target_one(1)
    for u in range(NY):
        loads[3 + u].wait()
        premix(tr_v, 16 * u, store_y(my.at[u]))
        step(u, 0)
    for u in range(NX):
        loads[3 + NY + u].wait()
        for k in range(2):
            premix(tr_v, 16 * NY + 32 * u + 16 * k, store_split(mx.at[u], k))
    send_x(0, FAR_FIRST + (0,))
    send_x(1, FAR_FIRST[:1])
    target_two(0)
    target_two(1)
    tables()
    for u in range(2):
        step(u, 1)
    target_across(0)
    for u in range(2, NY):
        step(u, 1)
    target_across(1)
    send_x(1, FAR_FIRST[1:] + (0,))
    for u in range(NX):
        step(NY + u, 0)
    for u in range(2):
        step(u, 2)
    pl.semaphore_wait(far_z, 2)
    target_finish(0)
    for u in range(2, NY):
        step(u, 2)
    target_finish(1)
    start(cc[0])
    for u in range(NX):
        step(NY + u, 1)
    for u in range(NY):
        step(u, 3)
    for u in range(NX):
        step(NY + u, 2)
    for u in range(NY):
        finish_y_send(u)
    for u in range(NX):
        step(NY + u, 3)
    for u in range(NY):
        finish_y(u)
    for u in range(NX):
        finish_x(NY + u)

    wide = proj[...].astype(F32)
    square = wide * wide
    high = square.astype(BF)
    low = (square - high.astype(F32)).astype(BF)
    ones = jnp.ones((8, W), BF)
    stat[...] = lax.dot_general(ones, high, NT, preferred_element_type=F32) + lax.dot_general(
        ones, low, NT, preferred_element_type=F32
    )
    for j in range(len(PEERS)):
        start(st[j])
    local = jnp.sum(square, axis=1, keepdims=True)
    scaled_t = (wide * lax.rsqrt(local * (1.0 / W) + 1e-30)).astype(BF).T
    for d in FAR_FIRST:
        forward(d)

    lane = lax.broadcasted_iota(jnp.int32, (256, 128), 1)
    squares = jnp.zeros((256, 128), F32)
    for k, pair in enumerate(PAIRS):
        for d in pair:
            cc[d].wait_recv()
        rows = jnp.concatenate([tall[d].reshape(128, W) for d in pair], axis=0)
        products = jnp.dot(rows, scaled_t, preferred_element_type=F32).astype(BF)
        ordered = jnp.dot(perm[...], products, preferred_element_type=F32).astype(BF)
        part[:, pl.ds(16 * k, 16), :] = ordered.reshape(NF, 16, TRAIN)
        wide = rows.astype(F32)
        norm = jnp.sum(wide * wide, axis=1, keepdims=True)
        norm_high = norm.astype(BF).astype(F32)
        squares = squares + jnp.where(lane == 2 * k, norm_high, 0.0) + jnp.where(lane == 2 * k + 1, norm - norm_high, 0.0)
        if k == len(PAIRS) - 1:
            moved = jnp.dot(perm[...], squares.astype(BF), preferred_element_type=F32).astype(BF)
            part[:, pl.ds(64, 16), :] = moved.reshape(NF, 16, 128)
        for r in range(ROUNDS):
            if GROUPS[r][-1] == k:
                for j in range(len(PEERS)):
                    start(co[r, j])

    sums = stat[...]
    for j in range(len(PEERS)):
        st[j].wait_recv()
        sums = sums + rstat[j]
    scale = lax.rsqrt(sums[0:1] * (1.0 / PROJ) + 1e-06)
    eye = lax.broadcasted_iota(jnp.int32, (TRAIN, TRAIN), 0) == lax.broadcasted_iota(jnp.int32, (TRAIN, TRAIN), 1)
    column = jnp.sum(jnp.where(eye, scale, 0.0), axis=1, keepdims=True)
    feat_out[...] = (proj[...].astype(F32) * column).astype(BF)

    def undo(sums):
        mean = sums[0:1] * (1.0 / W) + 1e-30
        return mean * lax.rsqrt(mean) * scale

    moved_sum = part[f, pl.ds(64, 16)].astype(F32)
    total = part[f, pl.ds(0, 64)].astype(F32) * undo(stat)
    for j in range(len(PEERS)):
        for r in range(ROUNDS):
            co[r, j].wait_recv()
        moved_sum = moved_sum + rpart[j, pl.ds(64, 16)].astype(F32)
        total = total + rpart[j, pl.ds(0, 64)].astype(F32) * undo(rstat[j])
    lane16 = lax.broadcasted_iota(jnp.int32, (16, 128), 1)
    for k, pair in enumerate(PAIRS):
        norm = jnp.sum(jnp.where(lane16 // 2 == k, moved_sum, 0.0), axis=1, keepdims=True)
        factor = lax.rsqrt(norm * (1.0 / PROJ) + 1e-06) * (1.0 / PROJ)
        block = total[16 * k : 16 * k + 16] * factor
        for i, d in enumerate(pair):
            cos_out[pl.ds(pl.multiple_of(((z + d) % 8) * 8, 8), 8), :] = block[8 * i : 8 * i + 8]

    for copy in sent:
        copy.wait_send()


def solution(mesh):
    vm = pltpu.VMEM
    dma = pltpu.SemaphoreType.DMA
    n_peers = len(PEERS)
    scratch = [
        vm((TRAIN, 2 * PROJ), BF), vm((32, 2 * PROJ), BF), vm((32, PROJ), jnp.int32), vm((8, PROJ), F32),
        vm((W, W), BF), vm((256, 256), BF),
        vm((2, 8, 32, W), BF), vm((2, 2, 16, W), BF), vm((2, 2, 3, 32, W), BF), vm((2, 2, 16, W), BF), vm((2, 3, 16, W), BF),
        vm((NY, 8, 32, W), BF), vm((NX, 2, 8, 32, W), BF), vm((NX, 8, 32, W), BF), vm((U, 2, 4, 32, W), BF),
        vm((NY, 2, 16, W), BF), vm((NY, 16, W), BF),
        vm((8, 2, 2, 2, 16, W), BF), vm((TRAIN, W), BF),
        vm((8, 128), F32), vm((n_peers, 8, 128), F32),
        vm((NF, 80, 128), BF), vm((n_peers, 80, 128), BF),
        dma((3 + U,)), dma((NX, 8)), dma((NX, 8)), dma((2, 2, 4)), dma((2, 2, 4)),
        dma((U, 2, 4)), dma((U, 2, 4)), dma((NY,)), dma((NY,)), dma((2, 3)), dma((2, 3)), dma((2, 8)), dma((2, 8)),
        dma((8,)), dma((8,)), dma((n_peers,)), dma((n_peers,)), dma((ROUNDS, n_peers)), dma((ROUNDS, n_peers)),
        pltpu.SemaphoreType.REGULAR,
    ]
    hbm = pl.BlockSpec(memory_space=pl.ANY)
    whole = pl.BlockSpec(memory_space=pltpu.VMEM)

    def local(train_grads, target_grads, signs, block_order):
        features, cosines = pl.pallas_call(
            kernel,
            out_shape=(
                jax.ShapeDtypeStruct((TRAIN, W), BF),
                jax.ShapeDtypeStruct((64, 128), F32),
            ),
            in_specs=[hbm, hbm, hbm, whole],
            out_specs=(whole, whole),
            scratch_shapes=scratch,
            compiler_params=pltpu.CompilerParams(
                collective_id=0, has_side_effects=True, vmem_limit_bytes=int(VML * 2**20)
            ),
        )(train_grads, target_grads, signs, block_order.reshape(1, 32))
        return features, cosines.reshape(32, 2, TRAIN).transpose(2, 0, 1)

    placed = (P("ex", "feat"), P("ex", "feat"), P(), P())
    return jax.shard_map(
        local,
        mesh=mesh,
        in_specs=placed,
        out_specs=(P("ex", "feat"), P("ex", None, "feat")),
        check_vma=False,
    )
```

time: 68.9 us -> 61 us (0.89)
  Pallas kernels: 63.7 us -> 58.3 us
  local copies, waits for them, and re-layouts: 4.37 us -> 1.92 us
    pallas_call x1, Pallas kernels: 63.7 us -> 58.3 us  [local(): pl.pallas_call(kernel, out_shape=(jax.ShapeDtypeStruct((TRAIN, W), BF), j...]
    unnamed x8 -> x4, local copies, waits for them, and re-layouts: 4.37 us -> 1.92 us
where the time goes in v2:
time: 61 us; the launch traced here: 60.8 us
  Pallas kernels  58.3 us (96%)
  local copies, waits for them, and re-layouts  1.92 us (3%)
  between operations  0.65 us (1%)
    pallas_call x1, Pallas kernels, local(): pl.pallas_call(kernel, out_shape=(jax.ShapeDtypeStruct((TRAIN, W), BF), j...  58.3 us
    unnamed x4, local copies, waits for them, and re-layouts  1.92 us

profile of v2, /device:TPU:1, one launch (start us, length us, event | category | flops | bytes accessed | tf_op | source)
XLA Modules:
  0.0 60.8 jit_solution(7115805379854185065)
XLA Ops:
  0.6 0.0 copy-start
  0.6 0.6 %copy-done = s32[32]{0:T(128)S(1)} copy-done((s32[32]{0:T(128)S(1)}, s32[32]{0:T(128)}, u32[]{:S(2)}) %copy-start) | copy-done | bytes 152
  1.3 58.3 %shard_map.59 = (bf16[128,512]{1,0:T(8,128)(2,1)S(1)}, f32[64,128]{1,0:T(8,128)S(1)}) custom-call(bf16[128,16384]{1,0:T(8,128)(2,1)} %train_hbm.1, bf16[32,16384]{1,0:T(8,128)(2,1)} %target_hbm.1, s32[32,8192]{1,0:T(8,128)} %signs_hbm.1, s32[1,32]{1,0:T(1,128)S(1)} %bitcast.5), custom_call_target="tpu_custom_call" | custom-call | tf_op jit(solution)/shard_map/pallas_call | solution.py:449
  59.6 0.7 %copy.8 = bf16[128,512]{1,0:T(8,128)(2,1)} copy(bf16[128,512]{1,0:T(8,128)(2,1)S(1)} %get-tuple-element.8) | data formatting | bytes 262144
  60.2 0.6 %copy.9 = f32[128,32,2]{0,2,1:T(2,128)} copy(f32[128,32,2]{0,2,1:T(2,128)S(1)} %bitcast.4) | data formatting | bytes 65536
Async XLA Ops:
  0.6 0.7 %copy-start = (s32[32]{0:T(128)S(1)}, s32[32]{0:T(128)}, u32[]{:S(2)}) copy-start(s32[32]{0:T(128)} %param.7) | copy-start | bytes 388

commit v3 on v2

--- a/solution.py
+++ b/solution.py
@@ -22,8 +22,6 @@
 NT = (((1,), (1,)), ((), ()))
 FAR_FIRST = (4, 3, 5, 2, 6, 1, 7)
 PAIRS = ((0, 4), (3, 5), (2, 6), (1, 7))
-GROUPS = ((0, 1, 2), (3,))
-ROUNDS = len(GROUPS)
 PEERS = tuple((a, d) for d in (4, 3, 5, 2, 6, 1, 7, 0) for a in (1, 0) if (a, d) != (0, 0))
 
 
@@ -44,8 +42,8 @@
     train_hbm, target_hbm, signs_hbm, order_ref,
     feat_out, cos_out,
     tr_v, tg_v, sg_v, lsig, had, perm,
-    mt, rt4, rt, zt, rzt, my, mx, rxx, rcv, zs, rzs, tall, proj, stat, rstat, part, rpart,
-    ld, xx_s, xx_r, ty_s, ty_r, it_s, it_r, yx_s, yx_r, tq_s, tq_r, zz_s, zz_r, cc_s, cc_r, st_s, st_r, co_s, co_r, far_z,
+    mt, rt4, rt, zt, rzt, my, mx, rxx, rcv, zs, rzs, tall, proj, stat, rstat, part, rpart, norms, rnorms,
+    ld, xx_s, xx_r, ty_s, ty_r, it_s, it_r, yx_s, yx_r, tq_s, tq_r, zz_s, zz_r, cc_s, cc_r, st_s, st_r, co_s, co_r, ct_s, ct_r, far_z,
 ):
     f = lax.axis_index("feat")
     e = lax.axis_index("ex")
@@ -193,11 +191,11 @@
         j: remote(stat, rstat.at[j], st_s.at[j], st_r.at[j], on_feat(a, d)) for j, (a, d) in enumerate(PEERS)
     }
     co = {}
-    for r in range(ROUNDS):
-        rows = pl.ds(16 * GROUPS[r][0], 16 * len(GROUPS[r]) + (0 if r + 1 < ROUNDS else 16))
-        for j, (a, d) in enumerate(PEERS):
-            dev = on_feat(a, d)
-            co[r, j] = remote(part.at[dev[0], rows], rpart.at[j, rows], co_s.at[r, j], co_r.at[r, j], dev)
+    ct = {}
+    for j, (a, d) in enumerate(PEERS):
+        dev = on_feat(a, d)
+        co[j] = remote(part.at[dev[0]], rpart.at[j], co_s.at[j], co_r.at[j], dev)
+        ct[j] = remote(norms.at[dev[0]], rnorms.at[j], ct_s.at[j], ct_r.at[j], dev)
 
     sent = []
 
@@ -290,6 +288,24 @@
         tall[0, c, k, 1 - xl] = done[16:32]
         for d in FAR_FIRST:
             start(zz[k, d])
+
+    def target_rows(pair):
+        return jnp.concatenate([tall[d].reshape(128, W) for d in pair], axis=0)
+
+    def target_norms():
+        lane = lax.broadcasted_iota(jnp.int32, (256, 128), 1)
+        squares = jnp.zeros((256, 128), F32)
+        for k, pair in enumerate(PAIRS):
+            for d in pair:
+                cc[d].wait_recv()
+            rows = target_rows(pair).astype(F32)
+            norm = jnp.sum(rows * rows, axis=1, keepdims=True)
+            high = norm.astype(BF).astype(F32)
+            squares = squares + jnp.where(lane == 2 * k, high, 0.0) + jnp.where(lane == 2 * k + 1, norm - high, 0.0)
+        moved = jnp.dot(perm[...], squares.astype(BF), preferred_element_type=F32).astype(BF)
+        norms[...] = moved.reshape(NF, 16, 128)
+        for j in range(len(PEERS)):
+            start(ct[j])
 
     def send_x(u, distances):
         for d in distances:
@@ -349,10 +365,15 @@
         step(NY + u, 2)
     for u in range(NY):
         finish_y_send(u)
+    for d in FAR_FIRST[:3]:
+        forward(d)
     for u in range(NX):
         step(NY + u, 3)
+    for d in FAR_FIRST[3:]:
+        forward(d)
     for u in range(NY):
         finish_y(u)
+    target_norms()
     for u in range(NX):
         finish_x(NY + u)
 
@@ -368,30 +389,16 @@
         start(st[j])
     local = jnp.sum(square, axis=1, keepdims=True)
     scaled_t = (wide * lax.rsqrt(local * (1.0 / W) + 1e-30)).astype(BF).T
-    for d in FAR_FIRST:
-        forward(d)
-
-    lane = lax.broadcasted_iota(jnp.int32, (256, 128), 1)
-    squares = jnp.zeros((256, 128), F32)
+
     for k, pair in enumerate(PAIRS):
-        for d in pair:
-            cc[d].wait_recv()
-        rows = jnp.concatenate([tall[d].reshape(128, W) for d in pair], axis=0)
-        products = jnp.dot(rows, scaled_t, preferred_element_type=F32).astype(BF)
+        products = jnp.dot(target_rows(pair), scaled_t, preferred_element_type=F32).astype(BF)
         ordered = jnp.dot(perm[...], products, preferred_element_type=F32).astype(BF)
         part[:, pl.ds(16 * k, 16), :] = ordered.reshape(NF, 16, TRAIN)
-        wide = rows.astype(F32)
-        norm = jnp.sum(wide * wide, axis=1, keepdims=True)
-        norm_high = norm.astype(BF).astype(F32)
-        squares = squares + jnp.where(lane == 2 * k, norm_high, 0.0) + jnp.where(lane == 2 * k + 1, norm - norm_high, 0.0)
-        if k == len(PAIRS) - 1:
-            moved = jnp.dot(perm[...], squares.astype(BF), preferred_element_type=F32).astype(BF)
-            part[:, pl.ds(64, 16), :] = moved.reshape(NF, 16, 128)
-        for r in range(ROUNDS):
-            if GROUPS[r][-1] == k:
-                for j in range(len(PEERS)):
-                    start(co[r, j])
-
+    for j in range(len(PEERS)):
+        start(co[j])
+
+    for copy in sent[: -len(PEERS)]:
+        copy.wait_send()
     sums = stat[...]
     for j in range(len(PEERS)):
         st[j].wait_recv()
@@ -403,24 +410,26 @@
 
     def undo(sums):
         mean = sums[0:1] * (1.0 / W) + 1e-30
-        return mean * lax.rsqrt(mean) * scale
-
-    moved_sum = part[f, pl.ds(64, 16)].astype(F32)
-    total = part[f, pl.ds(0, 64)].astype(F32) * undo(stat)
+        return mean * lax.rsqrt(mean)
+
+    norm_sum = norms[f].astype(F32)
     for j in range(len(PEERS)):
-        for r in range(ROUNDS):
-            co[r, j].wait_recv()
-        moved_sum = moved_sum + rpart[j, pl.ds(64, 16)].astype(F32)
-        total = total + rpart[j, pl.ds(0, 64)].astype(F32) * undo(rstat[j])
+        ct[j].wait_recv()
+        norm_sum = norm_sum + rnorms[j].astype(F32)
+    total = part[f].astype(F32) * undo(stat)
+    for j in range(len(PEERS)):
+        co[j].wait_recv()
+        total = total + rpart[j].astype(F32) * undo(rstat[j])
+    total = total * scale
     lane16 = lax.broadcasted_iota(jnp.int32, (16, 128), 1)
     for k, pair in enumerate(PAIRS):
-        norm = jnp.sum(jnp.where(lane16 // 2 == k, moved_sum, 0.0), axis=1, keepdims=True)
+        norm = jnp.sum(jnp.where(lane16 // 2 == k, norm_sum, 0.0), axis=1, keepdims=True)
         factor = lax.rsqrt(norm * (1.0 / PROJ) + 1e-06) * (1.0 / PROJ)
         block = total[16 * k : 16 * k + 16] * factor
         for i, d in enumerate(pair):
             cos_out[pl.ds(pl.multiple_of(((z + d) % 8) * 8, 8), 8), :] = block[8 * i : 8 * i + 8]
 
-    for copy in sent:
+    for copy in sent[-len(PEERS) :]:
         copy.wait_send()
 
 
@@ -436,10 +445,10 @@
         vm((NY, 2, 16, W), BF), vm((NY, 16, W), BF),
         vm((8, 2, 2, 2, 16, W), BF), vm((TRAIN, W), BF),
         vm((8, 128), F32), vm((n_peers, 8, 128), F32),
-        vm((NF, 80, 128), BF), vm((n_peers, 80, 128), BF),
+        vm((NF, 64, 128), BF), vm((n_peers, 64, 128), BF), vm((NF, 16, 128), BF), vm((n_peers, 16, 128), BF),
         dma((3 + U,)), dma((NX, 8)), dma((NX, 8)), dma((2, 2, 4)), dma((2, 2, 4)),
         dma((U, 2, 4)), dma((U, 2, 4)), dma((NY,)), dma((NY,)), dma((2, 3)), dma((2, 3)), dma((2, 8)), dma((2, 8)),
-        dma((8,)), dma((8,)), dma((n_peers,)), dma((n_peers,)), dma((ROUNDS, n_peers)), dma((ROUNDS, n_peers)),
+        dma((8,)), dma((8,)), dma((n_peers,)), dma((n_peers,)), dma((n_peers,)), dma((n_peers,)), dma((n_peers,)), dma((n_peers,)),
         pltpu.SemaphoreType.REGULAR,
     ]
     hbm = pl.BlockSpec(memory_space=pl.ANY)

time: 61 us -> 58.4 us (0.957)
  Pallas kernels: 58.3 us -> 55.7 us
    pallas_call x1, Pallas kernels: 58.3 us -> 55.7 us  [local(): pl.pallas_call(kernel, out_shape=(jax.ShapeDtypeStruct((TRAIN, W), BF), j...]
where the time goes in v3:
time: 58.4 us; the launch traced here: 58.2 us
  Pallas kernels  55.7 us (95%)
  local copies, waits for them, and re-layouts  1.92 us (3%)
  between operations  0.65 us (1%)
    pallas_call x1, Pallas kernels, local(): pl.pallas_call(kernel, out_shape=(jax.ShapeDtypeStruct((TRAIN, W), BF), j...  55.7 us
    unnamed x4, local copies, waits for them, and re-layouts  1.92 us

profile of v3, /device:TPU:1, one launch (start us, length us, event | category | flops | bytes accessed | tf_op | source)
XLA Modules:
  0.0 58.2 jit_solution(1385694764152477937)
XLA Ops:
  0.6 0.0 copy-start
  0.6 0.6 %copy-done = s32[32]{0:T(128)S(1)} copy-done((s32[32]{0:T(128)S(1)}, s32[32]{0:T(128)}, u32[]{:S(2)}) %copy-start) | copy-done | bytes 152
  1.3 55.7 %shard_map.59 = (bf16[128,512]{1,0:T(8,128)(2,1)S(1)}, f32[64,128]{1,0:T(8,128)S(1)}) custom-call(bf16[128,16384]{1,0:T(8,128)(2,1)} %train_hbm.1, bf16[32,16384]{1,0:T(8,128)(2,1)} %target_hbm.1, s32[32,8192]{1,0:T(8,128)} %signs_hbm.1, s32[1,32]{1,0:T(1,128)S(1)} %bitcast.5), custom_call_target="tpu_custom_call" | custom-call | tf_op jit(solution)/shard_map/pallas_call | solution.py:458
  56.9 0.7 %copy.8 = bf16[128,512]{1,0:T(8,128)(2,1)} copy(bf16[128,512]{1,0:T(8,128)(2,1)S(1)} %get-tuple-element.8) | data formatting | bytes 262144
  57.6 0.6 %copy.9 = f32[128,32,2]{0,2,1:T(2,128)} copy(f32[128,32,2]{0,2,1:T(2,128)S(1)} %bitcast.4) | data formatting | bytes 65536
Async XLA Ops:
  0.6 0.7 %copy-start = (s32[32]{0:T(128)S(1)}, s32[32]{0:T(128)}, u32[]{:S(2)}) copy-start(s32[32]{0:T(128)} %param.7) | copy-start | bytes 388
